TPU v7x, 32 devices: a whole 2x2x4 slice. The times are simulated.
32 devices in a mesh: dp: 2 (over x), tp: 4 (over z), sec: 4 (over y, core).
Axes of the slice: x: 2, y: 2, z: 4, core: 2. Of those that a mesh axis runs over, the one named last changes fastest.
Arguments:
- hidden_states: bfloat16 [4, 128, 8192], P(None, ('dp', 'sec')), may hold values from -6 to 6
- w_query: bfloat16 [8192, 8192], P(('dp', 'sec'), 'tp'), may hold values from -0.0625 to 0.0625
- w_keyval: bfloat16 [8192, 2048], P(('dp', 'sec'), 'tp'), may hold values from -0.0625 to 0.0625
- key_cache: bfloat16 [128, 16, 256, 128], P(('dp', 'sec'), 'tp'), may hold values from -200 to 200, as said below
- value_cache: bfloat16 [128, 16, 256, 128], P(('dp', 'sec'), 'tp'), may hold values from -6 to 6
- cache_begin: int32 [128], P(('dp', 'sec')), may hold values from 0 to 128
- cache_end: int32 [128], P(('dp', 'sec')), may hold values from 256 to 512
Outputs:
- handoff: bfloat16 [4, 128, 8192], P(None, 'dp', ('tp', 'sec'))
Inputs may be any that keep to these rules, and one draw needn't show every extreme that they name: `key_cache`: cached keys; largest magnitudes differ between draws.
All inputs are finite; a program needn't handle non-finite values.
Results may differ from a plain program's by a relative error of at most 0.04.
Values may be sent and summed in bfloat16 or wider, within the bound.
A program may use at most 64 MiB of HBM per device.

v0:
```python
import functools

import jax
import jax.numpy as jnp
import numpy as np
from jax import lax
from jax.experimental import pallas as pl
from jax.experimental.pallas import tpu as pltpu
from jax.sharding import PartitionSpec as P

THETA = 500000.0


def swapped(value, axis, stride):
    mask = 2**stride
    pairs = [(source, source ^ mask) for source in range(lax.axis_size(axis))]
    return lax.ppermute(value, axis, pairs)


def rotate(vector, positions):
    half = vector.shape[-1] // 2
    freq = THETA ** (-(jnp.arange(half, dtype=jnp.float32) * 2.0 / vector.shape[-1]))
    angle = positions[..., None] * freq
    angle = angle.reshape(positions.shape + (1,) * (vector.ndim - positions.ndim - 1) + (half,))
    cosine = jnp.cos(angle)
    sine = jnp.sin(angle)
    first = vector[..., :half]
    second = vector[..., half:]
    return jnp.concatenate(
        [first * cosine - second * sine, second * cosine + first * sine], axis=-1
    )


def make_accumulate(token_rows, pieces):
    return (
        jnp.dot(token_rows, pieces[0], preferred_element_type=jnp.float32),
        jnp.dot(token_rows, pieces[1], preferred_element_type=jnp.float32),
    )


def partial_attention(query, keys, values, live, score_scale):
    scores = (
        jnp.einsum("sbkgd,bkpd->sbkgp", query, keys, preferred_element_type=jnp.float32)
        * score_scale
    )
    live = jnp.broadcast_to(live, scores.shape)
    masked = jnp.where(live, scores, jnp.float32(-1e30))
    maxima = jnp.max(masked, axis=-1)
    expo = jnp.where(live, jnp.exp(masked - maxima[..., None]), jnp.float32(0.0))
    totals = jnp.sum(expo, axis=-1)
    weighted = jnp.einsum(
        "sbkgp,bkpd->sbkgd", expo.astype(jnp.bfloat16), values, preferred_element_type=jnp.float32
    )
    return (maxima, totals, weighted)


def merge_parts(parts):
    overall = parts[0][0]
    for entry in parts[1:]:
        overall = jnp.maximum(overall, entry[0])
    weighted = jnp.zeros_like(parts[0][2])
    totals = jnp.zeros_like(parts[0][1])
    for entry in parts:
        factor = jnp.exp(entry[0] - overall)
        weighted = weighted + entry[2] * factor[..., None]
        totals = totals + entry[1] * factor
    return weighted / totals[..., None]


def general_body(hidden_states, w_query, w_keyval, key_cache, value_cache, cache_begin, cache_end):
    num_steps, batch_rows, width = hidden_states.shape
    head_size = key_cache.shape[-1]
    query_cols = w_query.shape[1]
    keyval_cols = w_keyval.shape[1]
    local_heads = query_cols // head_size
    slot_count = key_cache.shape[1]
    half_len = key_cache.shape[2]
    score_scale = head_size ** (-0.5)
    sec_count = lax.axis_size("sec")
    sec_index = lax.axis_index("sec")
    sec_group = lax.all_gather(hidden_states, "sec", axis=1, tiled=True)
    shard_rows = w_query.shape[0]
    dp_count = width // (sec_count * shard_rows)
    group_rows = num_steps * batch_rows * sec_count
    grouped = sec_group.reshape(group_rows, dp_count, sec_count, shard_rows)
    chosen = lax.dynamic_slice_in_dim(grouped, sec_index, 1, 2).reshape(
        group_rows, dp_count * shard_rows
    )
    query_all, keyval_all = make_accumulate(
        chosen,
        (
            lax.all_gather(w_query, "dp", axis=0, tiled=True),
            lax.all_gather(w_keyval, "dp", axis=0, tiled=True),
        ),
    )
    query_acc, keyval_acc = (
        lax.psum_scatter(
            query_all.reshape(num_steps, sec_count * batch_rows, query_cols),
            "sec",
            scatter_dimension=1,
            tiled=True,
        ),
        lax.psum_scatter(
            keyval_all.reshape(num_steps, sec_count * batch_rows, keyval_cols),
            "sec",
            scatter_dimension=1,
            tiled=True,
        ),
    )
    query_acc = query_acc.reshape(num_steps * batch_rows, query_cols)
    keyval_acc = keyval_acc.reshape(num_steps * batch_rows, keyval_cols)
    positions = (
        cache_end.astype(jnp.float32)[None, :] + jnp.arange(num_steps, dtype=jnp.float32)[:, None]
    )
    query = rotate(
        query_acc.reshape(num_steps, batch_rows, local_heads, head_size), positions
    ).astype(jnp.bfloat16)
    step_ids = jnp.arange(num_steps, dtype=jnp.int32)
    causal = step_ids[None, :] <= step_ids[:, None]
    if slot_count == 1:
        parity = lax.axis_index("tp") % 2
        own_proj = keyval_acc.reshape(num_steps, batch_rows, head_size)
        own_proj = jnp.where(parity == 0, rotate(own_proj, positions), own_proj).astype(
            jnp.bfloat16
        )
        partner_query, partner_proj = swapped((query, own_proj), "tp", 0)
        new_keys = jnp.where(parity == 0, own_proj, partner_proj)
        new_values = jnp.where(parity == 0, partner_proj, own_proj)
        lower_heads = jnp.where(parity == 0, query, partner_query)
        upper_heads = jnp.where(parity == 0, partner_query, query)
        both_heads = jnp.concatenate([lower_heads, upper_heads], axis=2)[:, :, None]
        cache_pos = parity * half_len + jnp.arange(half_len, dtype=jnp.int32)
        cache_live = (cache_pos[None, :] >= cache_begin[:, None]) & (
            cache_pos[None, :] < cache_end[:, None]
        )
        cache_part = partial_attention(
            both_heads, key_cache, value_cache, cache_live[None, :, None, None, :], score_scale
        )
        mine_start = parity * local_heads
        theirs_start = (1 - parity) * local_heads

        def select_heads(array, start):
            return lax.dynamic_slice_in_dim(array, start, local_heads, 3)

        returned = (
            swapped(select_heads(cache_part[0], theirs_start).astype(jnp.bfloat16), "tp", 0).astype(
                jnp.float32
            ),
            swapped(select_heads(cache_part[1], theirs_start).astype(jnp.bfloat16), "tp", 0).astype(
                jnp.float32
            ),
            swapped(select_heads(cache_part[2], theirs_start).astype(jnp.bfloat16), "tp", 0).astype(
                jnp.float32
            ),
        )
        own_part = (
            select_heads(cache_part[0], mine_start),
            select_heads(cache_part[1], mine_start),
            select_heads(cache_part[2], mine_start),
        )
        fresh_part = partial_attention(
            query[:, :, None],
            jnp.transpose(new_keys, (1, 0, 2))[:, None],
            jnp.transpose(new_values, (1, 0, 2))[:, None],
            causal[:, None, None, None, :],
            score_scale,
        )
        parts = [own_part, returned, fresh_part]
    else:
        local_kv = keyval_cols // (2 * head_size)
        keyval = keyval_acc.reshape(num_steps, batch_rows, local_kv, 2, head_size)
        new_keys = rotate(keyval[:, :, :, 0], positions).astype(jnp.bfloat16)
        new_values = keyval[:, :, :, 1].astype(jnp.bfloat16)
        whole_keys = key_cache.reshape(batch_rows, local_kv, 2 * half_len, head_size)
        whole_values = value_cache.reshape(batch_rows, local_kv, 2 * half_len, head_size)
        grouped_query = query.reshape(
            num_steps, batch_rows, local_kv, local_heads // local_kv, head_size
        )
        cache_pos = jnp.arange(2 * half_len, dtype=jnp.int32)
        cache_live = (cache_pos[None, :] >= cache_begin[:, None]) & (
            cache_pos[None, :] < cache_end[:, None]
        )
        cache_part = partial_attention(
            grouped_query, whole_keys, whole_values, cache_live[None, :, None, None, :], score_scale
        )
        fresh_part = partial_attention(
            grouped_query,
            jnp.transpose(new_keys, (1, 2, 0, 3)),
            jnp.transpose(new_values, (1, 2, 0, 3)),
            causal[:, None, None, None, :],
            score_scale,
        )
        parts = [cache_part, fresh_part]
    attended = (
        merge_parts(parts)
        .astype(jnp.bfloat16)
        .reshape(num_steps, batch_rows, local_heads * head_size)
    )
    return lax.all_to_all(attended, "sec", split_axis=2, concat_axis=1, tiled=True)


def fused_kernel(
    group, freq_ref, begin_ref, end_ref, hidden_ref, wq_ref, wkv_ref, key_ref, value_ref, out_ref,
    xbuf, wbuf, pbuf, rbuf, kbuf, vbuf, cosine, sine, qbuf, fresh, obuf, abuf,
    x_local, x_send, x_recv, w_local, w_send, w_recv, kv_sem, r_send, r_recv, o_local, o_send, o_recv,
):
    chunks = wkv_ref.shape[1] // (2 * key_ref.shape[3])
    steps, batch, _ = hidden_ref.shape
    size = key_ref.shape[3]
    depth = wq_ref.shape[0]
    span = 2 * depth
    rows = steps * batch
    half_len = key_ref.shape[2]
    blocks = (group + 2) // 2
    wide = blocks * size
    dp, sec = lax.axis_index("dp"), lax.axis_index("sec")
    core = sec % 2
    dp_other = 1 - dp
    sec_far = (sec + 2) % 4
    sec_pair = sec + 1 - 2 * core
    near = ({"dp": dp, "sec": sec}, {"dp": dp_other, "sec": sec}, {"dp": dp, "sec": sec_far}, {"dp": dp_other, "sec": sec_far})
    pair = {"dp": dp, "sec": sec_pair}
    cross = {"dp": dp, "sec": (sec_pair + 2) % 4}
    odd = lax.axis_index("tp") % 2
    above = {"tp": lax.axis_index("tp") + 1 - 2 * odd}
    chips = (dp * 2 + sec // 2, dp_other * 2 + sec // 2, dp * 2 + sec_far // 2, dp_other * 2 + sec_far // 2)

    def weight_parts(chunk):
        first = chunk * group * size
        return (
            (2 * chunk, 0, wide, wq_ref, first),
            (2 * chunk + 1, 0, group * size - wide, wq_ref, first + wide),
            (2 * chunk + 1, group * size - wide, 2 * size, wkv_ref, chunk * 2 * size),
        )

    own_rows = pl.ds(pl.multiple_of(core * depth, depth), depth)

    def weight_refs(part):
        piece, start, width, source, column = part
        return (
            source.at[:, pl.ds(column, width)],
            wbuf.at[piece, own_rows, pl.ds(start, width)],
        )

    def hidden_slice(relation):
        return hidden_ref.at[:, :, pl.ds(pl.multiple_of(chips[relation] * span, span), span)]

    local_copies = {}
    x_own = pltpu.make_async_copy(hidden_slice(0), xbuf.at[0], x_local)
    x_own.start()
    for chunk in range(chunks):
        for index, part in enumerate(weight_parts(chunk)):
            source, target = weight_refs(part)
            copy = pltpu.make_async_copy(source, target, w_local.at[chunk, index])
            copy.start()
            local_copies[chunk, index] = copy

    barrier = pltpu.get_barrier_semaphore()
    for peer in near[1:] + (pair, cross, above):
        pl.semaphore_signal(barrier, inc=1, device_id=peer, device_id_type=pl.DeviceIdType.MESH)
    pl.semaphore_wait(barrier, 6)

    def deliver(source, target, index, device):
        return pltpu.make_async_remote_copy(
            src_ref=source, dst_ref=target, send_sem=x_send.at[index], recv_sem=x_recv.at[index],
            device_id=device, device_id_type=pl.DeviceIdType.MESH,
        )

    half_steps = steps // 2
    x_copies = []
    for step in range(half_steps):
        where = odd * half_steps + step
        x_copies.append(deliver(hidden_slice(3).at[where], xbuf.at[3, where], step, near[3]))
    for relation in (1, 2):
        x_copies.append(
            deliver(hidden_slice(relation), xbuf.at[relation], half_steps + relation - 1, near[relation])
        )
    for copy in x_copies:
        copy.start()
    w_copies = {}
    for chunk in range(chunks):
        for index, part in enumerate(weight_parts(chunk)):
            source, target = weight_refs(part)
            copy = pltpu.make_async_remote_copy(
                src_ref=source, dst_ref=target,
                send_sem=w_send.at[chunk, index], recv_sem=w_recv.at[chunk, index],
                device_id=pair, device_id_type=pl.DeviceIdType.MESH,
            )
            copy.start()
            w_copies[chunk, index] = copy
    kv_copies = []
    for chunk in range(chunks):
        slots = pl.ds(2 * chunk, 2)
        for index, (source, target) in enumerate(((key_ref, kbuf), (value_ref, vbuf))):
            copy = pltpu.make_async_copy(source.at[:, slots], target.at[chunk], kv_sem.at[chunk, index])
            copy.start()
            kv_copies.append(copy)

    row = lax.broadcasted_iota(jnp.int32, (rows, size), 0)
    lane = lax.broadcasted_iota(jnp.int32, (rows, size), 1)
    place = row // batch
    for index in range(batch):
        place = place + jnp.where(row % batch == index, end_ref[index], 0)
    angle = place.astype(jnp.float32) * freq_ref[...]
    cosine[...] = jnp.cos(angle)
    sine[...] = jnp.where(lane < size // 2, -jnp.sin(angle), jnp.sin(angle))

    def rotated(vector):
        return vector * cosine[...] + pltpu.roll(vector, size // 2, 1) * sine[...]

    def send(piece, message, source, target):
        copy = pltpu.make_async_remote_copy(
            src_ref=source, dst_ref=rbuf.at[piece, message],
            send_sem=r_send.at[piece, message], recv_sem=r_recv.at[piece, message],
            device_id=target, device_id_type=pl.DeviceIdType.MESH,
        )
        copy.start()
        return copy

    tile = 512 if span % 512 == 0 else span

    def multiply(piece, first, count):
        group_rows = pl.ds(first, count)
        for step in range(span // tile):
            deep = pl.ds(step * tile, tile)
            part = jnp.dot(
                xbuf[group_rows, :, :, deep].reshape(count * rows, tile), wbuf[piece, deep, :],
                preferred_element_type=jnp.float32,
            ).reshape(count, rows, wide)
            if step == 0:
                pbuf[piece, group_rows] = part
            else:
                pbuf[piece, group_rows] += part

    messages = {}

    def first_hop(piece, message):
        one = 1 if piece % 2 == 0 else 2
        source = pbuf.at[piece, 3 if message == 0 else one]
        messages[piece, message] = send(piece, message, source, near[one])

    def second_hop(piece):
        two = 2 if piece % 2 == 0 else 1
        messages[piece, 0].wait_recv()
        pbuf[piece, two] += rbuf[piece, 0]
        messages[piece, 2] = send(piece, 2, pbuf.at[piece, two], near[two])

    def await_weights(piece):
        for index in ((0,), (1, 2))[piece % 2]:
            local_copies[piece // 2, index].wait()
            w_copies[piece // 2, index].wait_recv()

    passed = []
    for step in range(half_steps):
        x_copies[step].wait_recv()
        here = xbuf.at[3, odd * half_steps + step]
        passed.append(deliver(here, here, half_steps + 2 + step, above))
        passed[-1].start()
    for step in range(half_steps):
        there = xbuf.at[3, (1 - odd) * half_steps + step]
        deliver(there, there, half_steps + 2 + step, above).wait_recv()
    for piece in range(2):
        await_weights(piece)
        multiply(piece, 3, 1)
        first_hop(piece, 0)
    x_own.wait()
    for copy in x_copies[half_steps:]:
        copy.wait_recv()
    for piece in range(2):
        multiply(piece, 0, 3)
        first_hop(piece, 1)
    def attend(chunk):
        new = [None, None]
        for half in range(2):
            piece = 2 * chunk + half
            messages[piece, 1].wait_recv()
            messages[piece, 2].wait_recv()
            for block in range(blocks):
                cols = pl.ds(block * size, size)
                total = pbuf[piece, 0, :, cols] + rbuf[piece, 1, :, cols] + rbuf[piece, 2, :, cols]
                head = half * blocks + block
                if head == group + 1:
                    new[1] = total.astype(jnp.bfloat16)
                elif head == group:
                    new[0] = rotated(total).astype(jnp.bfloat16)
                else:
                    turned = rotated(total).astype(jnp.bfloat16).astype(jnp.float32)
                    for step in range(steps):
                        qbuf[pl.ds(head * steps + step, batch, stride=group * steps), :] = turned[
                            step * batch : (step + 1) * batch
                        ]
        new_keys, new_values = new
        lines = group * steps
        scale = size ** (-0.5)
        query = qbuf[...].astype(jnp.bfloat16)
        contract = (((1,), (1,)), ((), ()))
        scores = lax.dot_general(query, new_keys, contract, preferred_element_type=jnp.float32) * scale
        line = lax.broadcasted_iota(jnp.int32, scores.shape, 0)
        other = lax.broadcasted_iota(jnp.int32, scores.shape, 1)
        live = (line // lines == other % batch) & (other // batch <= line % steps)
        fresh[...] = jnp.where(live, scores, jnp.float32(-1e30))
        kv_copies[2 * chunk].wait()
        kv_copies[2 * chunk + 1].wait()
        cache_len = 2 * half_len

        def one(index):
            here = pl.ds(pl.multiple_of(index * lines, lines), lines)
            keys = kbuf[chunk, index].reshape(cache_len, size)
            values = vbuf[chunk, index].reshape(cache_len, size)
            position = lax.broadcasted_iota(jnp.int32, (lines, cache_len), 1)
            cached = lax.dot_general(
                qbuf[here, :].astype(jnp.bfloat16), keys, contract, preferred_element_type=jnp.float32
            ) * scale
            cached = jnp.where(
                (position >= begin_ref[index]) & (position < end_ref[index]), cached, jnp.float32(-1e30)
            )
            extra = fresh[here, :]
            peak = jnp.maximum(
                jnp.max(cached, axis=1, keepdims=True), jnp.max(extra, axis=1, keepdims=True)
            )
            cached = jnp.exp(cached - peak)
            extra = jnp.exp(extra - peak)
            total = jnp.sum(cached, axis=1, keepdims=True) + jnp.sum(extra, axis=1, keepdims=True)
            weighted = jnp.dot(
                cached.astype(jnp.bfloat16), values, preferred_element_type=jnp.float32
            ) + jnp.dot(extra.astype(jnp.bfloat16), new_values, preferred_element_type=jnp.float32)
            obuf[here, :] = weighted / total

        unroll = 8 if batch % 8 == 0 else 1

        def several(outer, carry):
            for inner in range(unroll):
                one(outer * unroll + inner)
            return carry

        lax.fori_loop(0, batch // unroll, several, 0)
        for head in range(group):
            for step in range(steps):
                abuf[chunk, step, :, pl.ds(head * size, size)] = obuf[
                    pl.ds(head * steps + step, batch, stride=lines), :
                ].astype(jnp.bfloat16)

    share = out_ref.shape[2]
    per = 4 // chunks
    out_rows = pl.ds(pl.multiple_of(sec * batch, batch), batch)

    def handoff(target):
        chunk, place = target // per, target % per
        source = abuf.at[chunk, :, :, pl.ds(place * share, share)]
        keep = pltpu.make_async_copy(source, out_ref.at[:, out_rows, :], o_local)
        copy = pltpu.make_async_remote_copy(
            src_ref=source, dst_ref=out_ref.at[:, out_rows, :],
            send_sem=o_send.at[target], recv_sem=o_recv.at[sec],
            device_id={"dp": dp, "sec": target}, device_id_type=pl.DeviceIdType.MESH,
        )
        return keep, copy

    for piece in range(2):
        second_hop(piece)
    for chunk in range(chunks):
        if chunk + 1 < chunks:
            for piece in (2 * chunk + 2, 2 * chunk + 3):
                await_weights(piece)
                multiply(piece, 0, 4)
                first_hop(piece, 0)
                first_hop(piece, 1)
            second_hop(2 * chunk + 2)
            second_hop(2 * chunk + 3)
        attend(chunk)
        for target in range(chunk * per, (chunk + 1) * per):
            keep, copy = handoff(target)
            pl.when(sec == target)(keep.start)
            pl.when(sec != target)(copy.start)

    for target in range(4):
        keep, copy = handoff(target)
        pl.when(sec == target)(keep.wait)
        pl.when(sec != target)(copy.wait_send)
        arrived = pltpu.make_async_remote_copy(
            src_ref=abuf.at[0, :, :, pl.ds(0, share)],
            dst_ref=out_ref.at[:, pl.ds(target * batch, batch), :],
            send_sem=o_send.at[target], recv_sem=o_recv.at[target],
            device_id={"dp": dp, "sec": target}, device_id_type=pl.DeviceIdType.MESH,
        )
        pl.when(sec != target)(arrived.wait_recv)
    for copy in x_copies + passed + list(w_copies.values()) + list(messages.values()):
        copy.wait_send()


def fused_body(hidden_states, w_query, w_keyval, key_cache, value_cache, cache_begin, cache_end):
    steps, batch, _ = hidden_states.shape
    slots, half_len, size = key_cache.shape[1:]
    depth = w_query.shape[0]
    chunks = slots // 2
    group = w_query.shape[1] // size // chunks
    rows = steps * batch
    wide = (group + 2) // 2 * size
    pieces = 2 * chunks
    share = w_query.shape[1] // 4
    lanes = np.arange(size, dtype=np.float32) % (size // 2)
    freq = np.float32(THETA) ** (-(lanes * np.float32(2.0) / np.float32(size)))
    anywhere = pl.BlockSpec(memory_space=pl.ANY)
    scalars = pl.BlockSpec(memory_space=pltpu.SMEM)
    dma = pltpu.SemaphoreType.DMA
    return pl.pallas_call(
        functools.partial(fused_kernel, group),
        out_shape=jax.ShapeDtypeStruct((steps, 4 * batch, share), jnp.bfloat16),
        in_specs=[pl.BlockSpec(memory_space=pltpu.VMEM), scalars, scalars] + [anywhere] * 5,
        out_specs=anywhere,
        scratch_shapes=[
            pltpu.VMEM((4, steps, batch, 2 * depth), jnp.bfloat16),
            pltpu.VMEM((pieces, 2 * depth, wide), jnp.bfloat16),
            pltpu.VMEM((pieces, 4, rows, wide), jnp.float32),
            pltpu.VMEM((pieces, 3, rows, wide), jnp.float32),
            pltpu.VMEM((chunks, batch, 2, half_len, size), jnp.bfloat16),
            pltpu.VMEM((chunks, batch, 2, half_len, size), jnp.bfloat16),
            pltpu.VMEM((rows, size), jnp.float32),
            pltpu.VMEM((rows, size), jnp.float32),
            pltpu.VMEM((group * rows, size), jnp.float32),
            pltpu.VMEM((group * rows, rows), jnp.float32),
            pltpu.VMEM((group * rows, size), jnp.float32),
            pltpu.VMEM((chunks, steps, batch, group * size), jnp.bfloat16),
            dma, dma((steps + 2,)), dma((steps + 2,)),
            dma((chunks, 3)), dma((chunks, 3)), dma((chunks, 3)),
            dma((chunks, 2)),
            dma((pieces, 3)), dma((pieces, 3)),
            dma, dma((4,)), dma((4,)),
        ],
        compiler_params=pltpu.CompilerParams(
            collective_id=0, has_side_effects=True, vmem_limit_bytes=56 * 1024 * 1024
        ),
        cost_estimate=pl.CostEstimate(
            flops=2 * 4 * rows * 2 * depth * pieces * wide,
            bytes_accessed=2 * (w_query.size + w_keyval.size + 2 * key_cache.size),
            transcendentals=0,
        ),
    )(freq[None, :], cache_begin, cache_end, hidden_states, w_query, w_keyval, key_cache, value_cache)


def body(sizes, hidden_states, w_query, w_keyval, key_cache, value_cache, cache_begin, cache_end):
    arrays = (hidden_states, w_query, w_keyval, key_cache, value_cache, cache_begin, cache_end)
    slots = key_cache.shape[1]
    if sizes["dp"] == 2 and sizes["sec"] == 4 and sizes["tp"] % 2 == 0 and slots in (2, 4, 8):
        return fused_body(*arrays)
    return general_body(*arrays)


def solution(mesh):
    return jax.shard_map(
        functools.partial(body, mesh.shape),
        mesh=mesh,
        in_specs=(
            P(None, ("dp", "sec"), None),
            P(("dp", "sec"), "tp"),
            P(("dp", "sec"), "tp"),
            P(("dp", "sec"), "tp", None, None),
            P(("dp", "sec"), "tp", None, None),
            P(("dp", "sec")),
            P(("dp", "sec")),
        ),
        out_specs=P(None, "dp", ("tp", "sec")),
        check_vma=False,
    )
```

profile of v0, /device:TPU:0, one launch (start us, length us, event | category | flops | bytes accessed | tf_op | source)
XLA Modules:
  0.0 48.7 jit_solution(5055653036967091306)
XLA Ops:
  0.0 47.1 %shard_map.82 = bf16[4,64,512]{2,1,0:T(8,128)(2,1)} custom-call(f32[1,128]{1,0:T(1,128)} %constant.2.clone.freq_ref, s32[16]{0:T(128)} %begin_ref.1, s32[16]{0:T(128)} %end_ref.1, bf16[4,16,8192]{2,1,0:T(8,128)(2,1)} %hidden_ref.1, bf16[1024,2048]{1,0:T(8,128)(2,1)} %wq_ref.1, bf16[1024,512]{1,0:T(8,128)(2,1)} %wkv_ref.1, bf16[16,4,256,128]{3,2,1,0:T(8,128)(2,1)} %key_ref.1, ...), custom_call_target="tpu_custom_call" | custom-call | flops 2684354560 | bytes 13631488 | tf_op jit(solution)/shard_map/pallas_call | solution.py:505
  47.1 1.7 %copy.10 = bf16[4,64,512]{2,1,0:T(8,128)(2,1)} copy(bf16[4,64,512]{2,1,0:T(8,128)(2,1)} %shard_map.82) | data formatting | bytes 524288
where the time goes:
time: 48.9 us; the launch traced here: 48.7 us
  Pallas kernels  47.1 us (96%)
  local copies, waits for them, and re-layouts  1.67 us (3%)
    pallas_call x1, Pallas kernels, fused_body(): pl.pallas_call(functools.partial(fused_kernel, group), out_shape=jax.Shap...  47.1 us
    unnamed x1, local copies, waits for them, and re-layouts  1.67 us

commit v1 on v0

--- a/solution.py
+++ b/solution.py
@@ -201,14 +201,13 @@
 
 def fused_kernel(
     group, freq_ref, begin_ref, end_ref, hidden_ref, wq_ref, wkv_ref, key_ref, value_ref, out_ref,
-    xbuf, wbuf, pbuf, rbuf, kbuf, vbuf, cosine, sine, qbuf, fresh, obuf, abuf,
-    x_local, x_send, x_recv, w_local, w_send, w_recv, kv_sem, r_send, r_recv, o_local, o_send, o_recv,
+    xbuf, wbuf, pbuf, gbuf, sbuf, rbuf, kbuf, vbuf, cosine, sine, qbuf, fresh, obuf, abuf,
+    x_local, x_send, x_recv, w_local, s_send, s_recv, kv_sem, r_send, r_recv, o_local, o_send, o_recv,
 ):
     chunks = wkv_ref.shape[1] // (2 * key_ref.shape[3])
     steps, batch, _ = hidden_ref.shape
     size = key_ref.shape[3]
     depth = wq_ref.shape[0]
-    span = 2 * depth
     rows = steps * batch
     half_len = key_ref.shape[2]
     blocks = (group + 2) // 2
@@ -219,11 +218,14 @@
     sec_far = (sec + 2) % 4
     sec_pair = sec + 1 - 2 * core
     near = ({"dp": dp, "sec": sec}, {"dp": dp_other, "sec": sec}, {"dp": dp, "sec": sec_far}, {"dp": dp_other, "sec": sec_far})
-    pair = {"dp": dp, "sec": sec_pair}
-    cross = {"dp": dp, "sec": (sec_pair + 2) % 4}
+    dp_at = (dp, dp_other, dp, dp_other)
+    sec_at = (sec, sec, sec_far, sec_far)
+    sec_across = (sec_pair, sec_pair, (sec_pair + 2) % 4, (sec_pair + 2) % 4)
+    places = tuple(zip(dp_at + dp_at, sec_at + sec_across))
+    everyone = tuple({"dp": one, "sec": two} for one, two in places)
+    pair = everyone[4]
     odd = lax.axis_index("tp") % 2
     above = {"tp": lax.axis_index("tp") + 1 - 2 * odd}
-    chips = (dp * 2 + sec // 2, dp_other * 2 + sec // 2, dp * 2 + sec_far // 2, dp_other * 2 + sec_far // 2)
 
     def weight_parts(chunk):
         first = chunk * group * size
@@ -233,17 +235,16 @@
             (2 * chunk + 1, group * size - wide, 2 * size, wkv_ref, chunk * 2 * size),
         )
 
-    own_rows = pl.ds(pl.multiple_of(core * depth, depth), depth)
-
     def weight_refs(part):
         piece, start, width, source, column = part
         return (
             source.at[:, pl.ds(column, width)],
-            wbuf.at[piece, own_rows, pl.ds(start, width)],
+            wbuf.at[piece, :, pl.ds(start, width)],
         )
 
     def hidden_slice(relation):
-        return hidden_ref.at[:, :, pl.ds(pl.multiple_of(chips[relation] * span, span), span)]
+        block = places[relation][0] * 4 + places[relation][1]
+        return hidden_ref.at[:, :, pl.ds(pl.multiple_of(block * depth, depth), depth)]
 
     local_copies = {}
     x_own = pltpu.make_async_copy(hidden_slice(0), xbuf.at[0], x_local)
@@ -256,9 +257,9 @@
             local_copies[chunk, index] = copy
 
     barrier = pltpu.get_barrier_semaphore()
-    for peer in near[1:] + (pair, cross, above):
+    for peer in everyone[1:] + (above,):
         pl.semaphore_signal(barrier, inc=1, device_id=peer, device_id_type=pl.DeviceIdType.MESH)
-    pl.semaphore_wait(barrier, 6)
+    pl.semaphore_wait(barrier, 8)
 
     def deliver(source, target, index, device):
         return pltpu.make_async_remote_copy(
@@ -266,28 +267,22 @@
             device_id=device, device_id_type=pl.DeviceIdType.MESH,
         )
 
+    def deliver(source, target, index, device):
+        return pltpu.make_async_remote_copy(
+            src_ref=source, dst_ref=target, send_sem=x_send.at[index], recv_sem=x_recv.at[index],
+            device_id=device, device_id_type=pl.DeviceIdType.MESH,
+        )
+
     half_steps = steps // 2
-    x_copies = []
-    for step in range(half_steps):
-        where = odd * half_steps + step
-        x_copies.append(deliver(hidden_slice(3).at[where], xbuf.at[3, where], step, near[3]))
-    for relation in (1, 2):
-        x_copies.append(
-            deliver(hidden_slice(relation), xbuf.at[relation], half_steps + relation - 1, near[relation])
-        )
-    for copy in x_copies:
-        copy.start()
-    w_copies = {}
-    for chunk in range(chunks):
-        for index, part in enumerate(weight_parts(chunk)):
-            source, target = weight_refs(part)
-            copy = pltpu.make_async_remote_copy(
-                src_ref=source, dst_ref=target,
-                send_sem=w_send.at[chunk, index], recv_sem=w_recv.at[chunk, index],
-                device_id=pair, device_id_type=pl.DeviceIdType.MESH,
-            )
-            copy.start()
-            w_copies[chunk, index] = copy
+    mine = pl.ds(odd * half_steps, half_steps)
+    theirs = pl.ds((1 - odd) * half_steps, half_steps)
+    x_copies = {}
+    for relation in (7, 3, 5, 6, 1, 2, 4):
+        source, target = hidden_slice(relation), xbuf.at[relation]
+        if relation % 4 == 3:
+            source, target = source.at[mine], target.at[mine]
+        x_copies[relation] = deliver(source, target, relation, everyone[relation])
+        x_copies[relation].start()
     kv_copies = []
     for chunk in range(chunks):
         slots = pl.ds(2 * chunk, 2)
@@ -317,22 +312,38 @@
         copy.start()
         return copy
 
-    tile = 512 if span % 512 == 0 else span
-
-    def multiply(piece, first, count):
-        group_rows = pl.ds(first, count)
-        for step in range(span // tile):
+    tile = 512 if depth % 512 == 0 else depth
+
+    def multiply(piece, first, target):
+        group_rows = pl.ds(first, 4)
+        for step in range(depth // tile):
             deep = pl.ds(step * tile, tile)
             part = jnp.dot(
-                xbuf[group_rows, :, :, deep].reshape(count * rows, tile), wbuf[piece, deep, :],
+                xbuf[group_rows, :, :, deep].reshape(4 * rows, tile), wbuf[piece, deep, :],
                 preferred_element_type=jnp.float32,
-            ).reshape(count, rows, wide)
+            ).reshape(4, rows, wide)
             if step == 0:
-                pbuf[piece, group_rows] = part
+                target[piece] = part
             else:
-                pbuf[piece, group_rows] += part
-
-    messages = {}
+                target[piece] += part
+
+    messages, swaps = {}, {}
+
+    def swap(piece):
+        for index, part in enumerate((pl.ds(3, 1), pl.ds(0, 3))):
+            copy = pltpu.make_async_remote_copy(
+                src_ref=gbuf.at[piece, part], dst_ref=sbuf.at[piece, part],
+                send_sem=s_send.at[piece, index], recv_sem=s_recv.at[piece, index],
+                device_id=pair, device_id_type=pl.DeviceIdType.MESH,
+            )
+            copy.start()
+            swaps[piece, index] = copy
+
+    def join(piece, message):
+        swaps[piece, message].wait_recv()
+        part = (pl.ds(3, 1), pl.ds(0, 3))[message]
+        pbuf[piece, part] += sbuf[piece, part]
+        first_hop(piece, message)
 
     def first_hop(piece, message):
         one = 1 if piece % 2 == 0 else 2
@@ -348,27 +359,35 @@
     def await_weights(piece):
         for index in ((0,), (1, 2))[piece % 2]:
             local_copies[piece // 2, index].wait()
-            w_copies[piece // 2, index].wait_recv()
 
     passed = []
-    for step in range(half_steps):
-        x_copies[step].wait_recv()
-        here = xbuf.at[3, odd * half_steps + step]
-        passed.append(deliver(here, here, half_steps + 2 + step, above))
+    for order, relation in enumerate((7, 3)):
+        x_copies[relation].wait_recv()
+        here = xbuf.at[relation, mine]
+        passed.append(deliver(here, here, 8 + order, above))
         passed[-1].start()
-    for step in range(half_steps):
-        there = xbuf.at[3, (1 - odd) * half_steps + step]
-        deliver(there, there, half_steps + 2 + step, above).wait_recv()
+    for relation in (4, 5, 6):
+        x_copies[relation].wait_recv()
+    x_copies[1].wait_recv()
+    x_copies[2].wait_recv()
+    x_own.wait()
+    for order, relation in enumerate((7, 3)):
+        there = xbuf.at[relation, theirs]
+        deliver(there, there, 8 + order, above).wait_recv()
     for piece in range(2):
         await_weights(piece)
-        multiply(piece, 3, 1)
-        first_hop(piece, 0)
-    x_own.wait()
-    for copy in x_copies[half_steps:]:
-        copy.wait_recv()
+        multiply(piece, 4, gbuf)
+        swap(piece)
     for piece in range(2):
-        multiply(piece, 0, 3)
-        first_hop(piece, 1)
+        multiply(piece, 0, pbuf)
+        join(piece, 0)
+    for piece in range(2):
+        join(piece, 1)
+    for piece in range(2, 2 * chunks):
+        await_weights(piece)
+        multiply(piece, 4, gbuf)
+        swap(piece)
+
     def attend(chunk):
         new = [None, None]
         for half in range(2):
@@ -407,7 +426,7 @@
             here = pl.ds(pl.multiple_of(index * lines, lines), lines)
             keys = kbuf[chunk, index].reshape(cache_len, size)
             values = vbuf[chunk, index].reshape(cache_len, size)
-            position = lax.broadcasted_iota(jnp.int32, (lines, cache_len), 1)
+            position = lax.broadcasted_iota(jnp.int32, (1, cache_len), 1)
             cached = lax.dot_general(
                 qbuf[here, :].astype(jnp.bfloat16), keys, contract, preferred_element_type=jnp.float32
             ) * scale
@@ -460,10 +479,9 @@
     for chunk in range(chunks):
         if chunk + 1 < chunks:
             for piece in (2 * chunk + 2, 2 * chunk + 3):
-                await_weights(piece)
-                multiply(piece, 0, 4)
-                first_hop(piece, 0)
-                first_hop(piece, 1)
+                multiply(piece, 0, pbuf)
+                join(piece, 0)
+                join(piece, 1)
             second_hop(2 * chunk + 2)
             second_hop(2 * chunk + 3)
         attend(chunk)
@@ -483,7 +501,7 @@
             device_id={"dp": dp, "sec": target}, device_id_type=pl.DeviceIdType.MESH,
         )
         pl.when(sec != target)(arrived.wait_recv)
-    for copy in x_copies + passed + list(w_copies.values()) + list(messages.values()):
+    for copy in list(x_copies.values()) + passed + list(swaps.values()) + list(messages.values()):
         copy.wait_send()
 
 
@@ -508,8 +526,10 @@
         in_specs=[pl.BlockSpec(memory_space=pltpu.VMEM), scalars, scalars] + [anywhere] * 5,
         out_specs=anywhere,
         scratch_shapes=[
-            pltpu.VMEM((4, steps, batch, 2 * depth), jnp.bfloat16),
-            pltpu.VMEM((pieces, 2 * depth, wide), jnp.bfloat16),
+            pltpu.VMEM((8, steps, batch, depth), jnp.bfloat16),
+            pltpu.VMEM((pieces, depth, wide), jnp.bfloat16),
+            pltpu.VMEM((pieces, 4, rows, wide), jnp.float32),
+            pltpu.VMEM((pieces, 4, rows, wide), jnp.float32),
             pltpu.VMEM((pieces, 4, rows, wide), jnp.float32),
             pltpu.VMEM((pieces, 3, rows, wide), jnp.float32),
             pltpu.VMEM((chunks, batch, 2, half_len, size), jnp.bfloat16),
@@ -520,8 +540,8 @@
             pltpu.VMEM((group * rows, rows), jnp.float32),
             pltpu.VMEM((group * rows, size), jnp.float32),
             pltpu.VMEM((chunks, steps, batch, group * size), jnp.bfloat16),
-            dma, dma((steps + 2,)), dma((steps + 2,)),
-            dma((chunks, 3)), dma((chunks, 3)), dma((chunks, 3)),
+            dma, dma((10,)), dma((10,)),
+            dma((chunks, 3)), dma((pieces, 2)), dma((pieces, 2)),
             dma((chunks, 2)),
             dma((pieces, 3)), dma((pieces, 3)),
             dma, dma((4,)), dma((4,)),

time: 48.9 us -> 52.2 us (1.067)
  Pallas kernels: 47.1 us -> 50.3 us
    pallas_call x1, Pallas kernels: 47.1 us -> 50.3 us  [fused_body(): pl.pallas_call(functools.partial(fused_kernel, group), out_shape=jax.Shap...]
where the time goes in v1:
time: 52.2 us; the launch traced here: 52 us
  Pallas kernels  50.3 us (96%)
  local copies, waits for them, and re-layouts  1.67 us (3%)
    pallas_call x1, Pallas kernels, fused_body(): pl.pallas_call(functools.partial(fused_kernel, group), out_shape=jax.Shap...  50.3 us
    unnamed x1, local copies, waits for them, and re-layouts  1.67 us

profile of v1, /device:TPU:0, one launch (start us, length us, event | category | flops | bytes accessed | tf_op | source)
XLA Modules:
  0.0 52.0 jit_solution(17501754011197825295)
XLA Ops:
  0.0 50.3 %shard_map.82 = bf16[4,64,512]{2,1,0:T(8,128)(2,1)} custom-call(f32[1,128]{1,0:T(1,128)} %constant.2.clone.freq_ref, s32[16]{0:T(128)} %begin_ref.1, s32[16]{0:T(128)} %end_ref.1, bf16[4,16,8192]{2,1,0:T(8,128)(2,1)} %hidden_ref.1, bf16[1024,2048]{1,0:T(8,128)(2,1)} %wq_ref.1, bf16[1024,512]{1,0:T(8,128)(2,1)} %wkv_ref.1, bf16[16,4,256,128]{3,2,1,0:T(8,128)(2,1)} %key_ref.1, ...), custom_call_target="tpu_custom_call" | custom-call | flops 2684354560 | bytes 13631488 | tf_op jit(solution)/shard_map/pallas_call | solution.py:523
  50.3 1.7 %copy.10 = bf16[4,64,512]{2,1,0:T(8,128)(2,1)} copy(bf16[4,64,512]{2,1,0:T(8,128)(2,1)} %shard_map.82) | data formatting | bytes 524288
